TPU v7x, 32 devices: a whole 2x2x4 slice. The times are simulated.
32 devices in a mesh: groups: 1, ctx: 32 (over z, y, x, core).
Axes of the slice: x: 2, y: 2, z: 4, core: 2. Of those that a mesh axis runs over, the one named last changes fastest.
Arguments:
- hidden_in: bfloat16 [4096, 4096], P(('groups', 'ctx')), may hold values from -64 to 64
- in_weight: bfloat16 [32, 128, 384], replicated, may hold values from -0.5 to 0.5
- feat_filter: float32 [3, 12288], replicated, may hold values from -3 to 3
- inner_filter: float32 [7, 4096], replicated, may hold values from -3 to 3
- norm_gain: float32 [4096], replicated, may hold values from 0.5 to 1.5
- attn_weight: bfloat16 [3, 32, 128, 128], replicated, may hold values from -3 to 3, as said below
- doc_lengths: int32 [8], P('groups'), may hold values from 1 to 8, as said below
Outputs:
- output: bfloat16 [4096, 4096], P(('groups', 'ctx'))
Inputs may be any that keep to these rules, and one draw needn't show every extreme that they name: Documents start at 128 times the running sums of doc_lengths and fill the sequence; the longest document is exactly 1024 tokens. `attn_weight`: Query, key and value maps in that order along the first dimension.
All inputs are finite; a program needn't handle non-finite values.
Results may differ from a plain program's by a relative error of at most 0.006.
The roundings to bfloat16 on the way count: a program that leaves them out, or rounds other values in their place, can miss the bound.
Values may be sent and summed in bfloat16 or wider, within the bound.
A program may use at most 128 MiB of HBM per device.

v0:
```python
import jax
import jax.numpy as jnp
from jax import lax
from jax.sharding import PartitionSpec as P

BLOCK = 128
REACH = 7


def shifted_2(block, axis, distance):
    devices = range(lax.axis_size(axis))
    route = [(i - distance, i) for i in devices if i - distance in devices]
    return lax.ppermute(block, axis, route)


def doc_start(positions, doc_lengths):
    doc_ends = jnp.cumsum(doc_lengths) * BLOCK
    passed = doc_ends[None, :] <= positions[:, None]
    return jnp.sum(jnp.where(passed, doc_lengths[None, :] * BLOCK, 0), axis=1)


def causal_taps(series, filter_taps, out_positions, out_begin):
    tap_count = filter_taps.shape[0]
    out_count = out_positions.shape[0]
    summed = jnp.zeros((out_count, series.shape[1]), jnp.float32)
    for shift_by in range(tap_count):
        shifted = series[tap_count - 1 - shift_by : tap_count - 1 - shift_by + out_count].astype(
            jnp.float32
        )
        allowed = (out_positions - shift_by >= out_begin)[:, None]
        summed = summed + jnp.where(allowed, shifted * filter_taps[shift_by][None, :], 0.0)
    return summed


def project_streams(tok_block, in_weight):
    out_count = tok_block.shape[0]
    head_count = in_weight.shape[0]
    head_dim = in_weight.shape[1]
    streams = jnp.einsum(
        "thd,hde->the",
        tok_block.reshape(out_count, head_count, head_dim),
        in_weight,
        preferred_element_type=jnp.float32,
    )
    return streams.astype(jnp.bfloat16).reshape(out_count, head_count * 3 * head_dim)


def attend(query_group, key_group, value_group, visible):
    scores = jnp.einsum(
        "thd,lhd->htl", query_group, key_group, preferred_element_type=jnp.float32
    ) * query_group.shape[2] ** (-0.5)
    scores = jnp.where(visible[None], scores, -1e30)
    row_top = jnp.max(scores, axis=-1, keepdims=True)
    exps = jnp.exp(scores - row_top)
    summed = jnp.sum(exps, axis=-1)
    weights_bf = exps.astype(jnp.bfloat16)
    attended = jnp.einsum(
        "htl,lhd->thd", weights_bf, value_group, preferred_element_type=jnp.float32
    )
    return attended / jnp.transpose(summed)[:, :, None]


def shards(hidden_in, in_weight, feat_filter, inner_filter, norm_gain, attn_weight, doc_lengths):
    tok_rows = hidden_in.shape[0]
    channels = hidden_in.shape[1]
    head_count = in_weight.shape[0]
    head_dim = in_weight.shape[1]
    feat_taps = feat_filter.shape[0]
    inner_taps = inner_filter.shape[0]
    anchor = lax.axis_index("ctx") * tok_rows
    positions = anchor + jnp.arange(tok_rows, dtype=jnp.int32)
    doc_begin = doc_start(positions, doc_lengths)
    streams = project_streams(hidden_in, in_weight)
    stream_edge = shifted_2(streams[tok_rows - (feat_taps - 1) :], "ctx", 1)
    features = causal_taps(
        jnp.concatenate([stream_edge, streams], axis=0), feat_filter, positions, doc_begin
    )
    features = features.reshape(tok_rows, head_count, 3, head_dim)
    own_gated = (
        (features[:, :, 1] * features[:, :, 2]).astype(jnp.bfloat16).reshape(tok_rows, channels)
    )
    gated_edge = shifted_2(own_gated[tok_rows - (inner_taps - 1) :], "ctx", 1)
    gated_rows = jnp.concatenate([gated_edge, own_gated], axis=0)
    query_h = features[:, :, 0].reshape(tok_rows, channels)
    convolved = causal_taps(gated_rows, inner_filter, positions, doc_begin)
    residual = (hidden_in.astype(jnp.float32) + query_h * convolved).astype(jnp.bfloat16)
    res_float = residual.astype(jnp.float32)
    normed = (
        res_float
        * lax.rsqrt(jnp.mean(res_float * res_float, axis=-1, keepdims=True) + 1e-05)
        * norm_gain[None, :]
    ).astype(jnp.bfloat16)
    projected = jnp.einsum(
        "thd,shde->sthe",
        normed.reshape(tok_rows, head_count, head_dim),
        attn_weight,
        preferred_element_type=jnp.float32,
    ).astype(jnp.bfloat16)
    kv_pair = projected[1:].reshape(2, tok_rows, channels)
    collected = [kv_pair]
    latest = kv_pair
    for offset in range(REACH):
        latest = shifted_2(latest, "ctx", 1)
        collected.append(latest)
    held_tiles = jnp.stack(collected, axis=0)
    window = jnp.flip(held_tiles, axis=0)
    key_rows = window[:, 0].reshape(-1, head_count, head_dim)
    value_rows = window[:, 1].reshape(-1, head_count, head_dim)
    key_pos = anchor - REACH * tok_rows + jnp.arange((REACH + 1) * tok_rows, dtype=jnp.int32)
    visible = (key_pos[None, :] >= doc_begin[:, None]) & (key_pos[None, :] <= positions[:, None])
    queries = projected[0]
    group_size = min(8, head_count)
    outputs = []
    for group_first in range(0, head_count, group_size):
        query_group = queries[:, group_first : group_first + group_size]
        key_group = key_rows[:, group_first : group_first + group_size]
        value_group = value_rows[:, group_first : group_first + group_size]
        outputs.append(attend(query_group, key_group, value_group, visible))
    attended = jnp.concatenate(outputs, axis=1).reshape(tok_rows, channels)
    return (res_float + attended).astype(jnp.bfloat16)


def solution(mesh):
    return jax.shard_map(
        shards,
        mesh=mesh,
        in_specs=(P(("groups", "ctx"), None), P(), P(), P(), P(), P(), P("groups")),
        out_specs=P(("groups", "ctx"), None),
        check_vma=False,
    )
```

profile of v0, /device:TPU:24, one launch (start us, length us, event | category | flops | bytes accessed | tf_op | source)
XLA Modules:
  0.0 377.1 jit_solution(10689706631848373150)
XLA Ops:
  0.0 1.9 copy-done
  1.9 2.3 convolution_convert_fusion
  4.2 2.7 slice.173
  6.9 3.4 copy.74
  10.2 1.9 collective-permute-start
  12.6 4.9 %collective-permute-done = bf16[2,12288]{1,0:T(2,128)(2,1)} collective-permute-done((bf16[2,12288]{1,0:T(2,128)(2,1)S(1)}, bf16[2,12288]{1,0:T(2,128)(2,1)}, u32[]{:S(2)}, u32[]{:S(2)}) %collective-permute-start) | collective-permute-done | bytes 49184 | tf_op jit(solution)/shard_map/ppermute | solution.py:13
  17.5 3.5 copy.75
  21.1 10.0 %select_add_fusion = f32[128,12288]{0,1:T(8,128)S(1)} fusion(bf16[128,12288]{0,1:T(8,128)(2,1)S(1)} %bitcast.110, bf16[2,12288]{0,1:T(8,128)(2,1)} %copy.75, f32[12288]{0:T(1024)S(1)} %bitcast.123, f32[12288]{0:T(1024)S(1)} %bitcast.124, f32[12288]{0:T(1024)S(1)} %bitcast.122, pred[128]{0:T(512)(128)(4,1)S(1)} %get-tuple-element.37, ...), kind=kLoop, calls=%fused_computation.2 | loop fusion | flops 26738688 | bytes 9634176 | tf_op jit(solution)/shard_map/add | solution.py:31
  31.1 2.7 fusion.97
  33.8 2.4 copy.108
  36.2 3.1 copy.109
  39.4 2.1 multiply_convert_fusion
  41.5 1.9 collective-permute-start.1
  43.6 1.4 copy.144
  45.0 1.9 copy.114
  46.9 2.0 collective-permute-done.1
  48.9 7.1 %fusion.17 = (f32[128]{0:T(128)S(1)}, bf16[128,4096]{1,0:T(8,128)(2,1)S(1)}) fusion(f32[128,4096]{1,0:T(8,128)S(1)} %copy.114, f32[4096]{0:T(1024)S(1)} %bitcast.130, bf16[128,4096]{1,0:T(8,128)(2,1)} %bitcast.121, bf16[6,4096]{1,0:T(8,128)(2,1)S(1)} %collective-permute-done.1, pred[128]{0:T(512)(128)(4,1)S(1)} %get-tuple-element.34, f32[4096]{0:T(1024)S(1)} %bitcast.131, ...), kind=kLoop, calls=%fused_computation.37 | loop fusion | flops 27262848 | bytes 5408128 | tf_op jit(solution)/shard_map/reduce_sum | solution.py:90
  56.1 0.4 fusion.77
  56.8 1.6 copy-done.9
  58.4 1.3 convert_bitcast_fusion
  60.1 1.2 copy-done.5
  61.3 1.9 collective-permute-start.2
  63.2 27.2 %collective-permute-done.2 = bf16[2,128,4096]{1,2,0:T(8,128)(2,1)S(1)} collective-permute-done((bf16[2,128,4096]{1,2,0:T(8,128)(2,1)S(1)}, bf16[2,128,4096]{1,2,0:T(8,128)(2,1)S(1)}, u32[]{:S(2)}, u32[]{:S(2)}) %collective-permute-start.2) | collective-permute-done | bytes 2097184 | tf_op jit(solution)/shard_map/ppermute | solution.py:13
  90.4 1.3 copy-done.10
  91.8 1.9 collective-permute-start.3
  93.7 27.2 %collective-permute-done.3 = bf16[2,128,4096]{1,2,0:T(8,128)(2,1)S(1)} collective-permute-done((bf16[2,128,4096]{1,2,0:T(8,128)(2,1)S(1)}, bf16[2,128,4096]{1,2,0:T(8,128)(2,1)S(1)}, u32[]{:S(2)}, u32[]{:S(2)}) %collective-permute-start.3) | collective-permute-done | bytes 2097184 | tf_op jit(solution)/shard_map/ppermute | solution.py:13
  120.9 1.3 copy-done.12
  122.2 1.9 collective-permute-start.4
  124.1 27.2 %collective-permute-done.4 = bf16[2,128,4096]{1,2,0:T(8,128)(2,1)S(1)} collective-permute-done((bf16[2,128,4096]{1,2,0:T(8,128)(2,1)S(1)}, bf16[2,128,4096]{1,2,0:T(8,128)(2,1)S(1)}, u32[]{:S(2)}, u32[]{:S(2)}) %collective-permute-start.4) | collective-permute-done | bytes 2097184 | tf_op jit(solution)/shard_map/ppermute | solution.py:13
  151.4 1.3 copy-done.14
  152.7 1.9 collective-permute-start.5
  154.6 27.3 %collective-permute-done.5 = bf16[2,128,4096]{1,2,0:T(8,128)(2,1)} collective-permute-done((bf16[2,128,4096]{1,2,0:T(8,128)(2,1)S(1)}, bf16[2,128,4096]{1,2,0:T(8,128)(2,1)}, u32[]{:S(2)}, u32[]{:S(2)}) %collective-permute-start.5) | collective-permute-done | bytes 2097184 | tf_op jit(solution)/shard_map/ppermute | solution.py:13
  181.9 2.1 collective-permute-start.6
  184.4 27.0 %collective-permute-done.6 = bf16[2,128,4096]{1,2,0:T(8,128)(2,1)} collective-permute-done((bf16[2,128,4096]{1,2,0:T(8,128)(2,1)}, bf16[2,128,4096]{1,2,0:T(8,128)(2,1)}, u32[]{:S(2)}, u32[]{:S(2)}) %collective-permute-start.6) | collective-permute-done | bytes 2097184 | tf_op jit(solution)/shard_map/ppermute | solution.py:13
  211.4 1.9 collective-permute-start.7
  213.3 0.3 bitcast_dynamic-update-slice_fusion.6
  213.6 0.3 bitcast_dynamic-update-slice_fusion.5
  213.9 1.3 copy-done.15
  215.5 25.3 %collective-permute-done.7 = bf16[2,128,4096]{1,2,0:T(8,128)(2,1)S(1)} collective-permute-done((bf16[2,128,4096]{1,2,0:T(8,128)(2,1)}, bf16[2,128,4096]{1,2,0:T(8,128)(2,1)S(1)}, u32[]{:S(2)}, u32[]{:S(2)}) %collective-permute-start.7) | collective-permute-done | bytes 2097184 | tf_op jit(solution)/shard_map/ppermute | solution.py:13
  240.7 1.9 collective-permute-start.8
  242.7 1.9 bitcast_dynamic-update-slice_fusion.3
  244.5 1.9 bitcast_dynamic-update-slice_fusion.2
  246.7 23.2 %collective-permute-done.8 = bf16[2,128,4096]{1,2,0:T(8,128)(2,1)S(1)} collective-permute-done((bf16[2,128,4096]{1,2,0:T(8,128)(2,1)S(1)}, bf16[2,128,4096]{1,2,0:T(8,128)(2,1)S(1)}, u32[]{:S(2)}, u32[]{:S(2)}) %collective-permute-start.8) | collective-permute-done | bytes 2097184 | tf_op jit(solution)/shard_map/ppermute | solution.py:13
  270.2 6.1 %fusion.95 = (bf16[8,1,128,4096]{2,3,1,0:T(8,128)(2,1)}, bf16[8,1,128,4096]{2,3,1,0:T(8,128)(2,1)}) fusion(bf16[8,2,128,4096]{2,3,1,0:T(8,128)(2,1)S(1)} %bitcast_dynamic-update-slice_fusion), kind=kLoop, calls=%fused_computation.127 | loop fusion | bytes 33554432 | tf_op jit(solution)/shard_map/slice | solution.py:107
  276.2 7.2 %slice.162 = bf16[8,1,128,4096]{2,3,1,0:T(8,128)(2,1)} reverse(bf16[8,1,128,4096]{2,3,1,0:T(8,128)(2,1)} %get-tuple-element.14), dimensions={0} | reverse | bytes 16777216 | tf_op jit(solution)/shard_map/slice | solution.py:107
  283.4 12.0 %copy.86 = bf16[8,1,128,4096]{3,2,0,1:T(8,128)(2,1)} copy(bf16[8,1,128,4096]{2,3,1,0:T(8,128)(2,1)} %slice.162) | data formatting | bytes 16777216 | tf_op jit(solution)/shard_map/slice | solution.py:107
  295.4 9.5 %copy.119 = bf16[128,8,32,128]{3,2,1,0:T(8,128)(2,1)} copy(bf16[128,8,32,128]{3,1,2,0:T(8,128)(2,1)} %bitcast.108) | data formatting | bytes 16777216
  304.9 5.5 %fusion.96 = (bf16[1024,8,128]{2,1,0:T(8,128)(2,1)S(1)}, bf16[1024,8,128]{2,1,0:T(8,128)(2,1)}, bf16[1024,8,128]{2,1,0:T(8,128)(2,1)}, bf16[1024,8,128]{2,1,0:T(8,128)(2,1)S(1)}) fusion(bf16[1024,32,128]{2,1,0:T(8,128)(2,1)} %bitcast.107), kind=kLoop, calls=%fused_computation.128 | loop fusion | bytes 16777216 | tf_op jit(solution)/shard_map/slice | solution.py:116
  310.4 2.7 fusion.31
  313.2 2.7 fusion.29
  315.8 7.2 %slice.157 = bf16[8,1,128,4096]{2,3,1,0:T(8,128)(2,1)} reverse(bf16[8,1,128,4096]{2,3,1,0:T(8,128)(2,1)} %get-tuple-element.15), dimensions={0} | reverse | bytes 16777216 | tf_op jit(solution)/shard_map/slice | solution.py:108
  323.1 10.3 %copy.85 = bf16[8,1,128,4096]{2,0,3,1:T(8,128)(2,1)} copy(bf16[8,1,128,4096]{2,3,1,0:T(8,128)(2,1)} %slice.157) | data formatting | bytes 16777216 | tf_op jit(solution)/shard_map/slice | solution.py:108
  333.4 13.4 %reshape_squeeze.10 = bf16[1024,32,128]{0,2,1:T(8,128)(2,1)} reshape(bf16[8,1,128,4096]{2,0,3,1:T(8,128)(2,1)} %copy.85) | data formatting | bytes 16777216 | tf_op jit(solution)/shard_map/reshape;squeeze | solution.py:108
  346.8 5.0 %fusion = (f32[8,128]{1,0:T(8,128)S(1)}, f32[8,128,1024]{2,1,0:T(8,128)}) fusion(pred[128,1024]{1,0:T(8,128)(4,1)S(1)} %compare_and_fusion, bf16[1024,8,128]{2,1,0:T(8,128)(2,1)} %get-tuple-element.18, bf16[3,128,32,128]{1,3,0,2:T(8,128)(2,1)S(1)} %copy-done.6), kind=kOutput, calls=%fused_computation.11 | convolution fusion | flops 271580160 | bytes 7475200 | tf_op jit(solution)/shard_map/thd,lhd->htl/dot_general | solution.py:49
  351.8 1.2 copy-done.16
  353.0 5.6 %fusion.4 = (f32[8,128]{1,0:T(8,128)S(1)}, f32[8,128]{1,0:T(8,128)S(1)}, f32[8,128]{1,0:T(8,128)S(1)}, f32[8,128]{1,0:T(8,128)S(1)}, f32[8,128,1024]{2,1,0:T(8,128)S(1)}) fusion(f32[8,128,1024]{2,1,0:T(8,128)} %get-tuple-element.41, f32[8,128]{1,0:T(8,128)S(1)} %get-tuple-element.40, pred[128,1024]{1,0:T(8,128)(4,1)S(1)} %compare_and_fusion, ...), kind=kOutput, calls=%fused_computation.15 | convolution fusion | flops 282062848 | bytes 20074496 | tf_op jit(solution)/shard_map/thd,lhd->htl/dot_general | solution.py:49
  358.6 3.5 fusion.74
  362.1 3.4 fusion.6
  365.5 1.3 fusion.71
  366.8 1.3 fusion.68
  368.1 1.3 fusion.65
  369.4 1.6 pad_maximum_fusion.1
  371.0 3.1 copy.95
  374.1 3.0 fusion.20
  (59 shorter events, 2.4 us)
Async XLA Ops:
  0.0 1.9 copy-start
  4.2 2.7 copy-start.2
  6.9 5.3 %copy-start.20 = (s32[8]{0:T(128)S(1)}, s32[8]{0:T(128)}, u32[]{:S(2)}) copy-start(s32[8]{0:T(128)} %param.13) | copy-start | bytes 100
  6.9 5.5 %copy-start.17 = (f32[3,12288]{1,0:T(4,128)S(1)}, f32[3,12288]{1,0:T(4,128)}, u32[]{:S(2)}) copy-start(f32[3,12288]{1,0:T(4,128)} %param.9) | copy-start | bytes 442372
  6.9 14.2 %copy-start.3 = (bf16[32,384,128]{2,1,0:T(8,128)(2,1)S(1)}, bf16[32,384,128]{2,1,0:T(8,128)(2,1)}, u32[]{:S(2)}) copy-start(bf16[32,384,128]{2,1,0:T(8,128)(2,1)} %copy-done.2) | copy-start | bytes 9437188
  10.2 7.3 %collective-permute-start = (bf16[2,12288]{1,0:T(2,128)(2,1)S(1)}, bf16[2,12288]{1,0:T(2,128)(2,1)}, u32[]{:S(2)}, u32[]{:S(2)}) collective-permute-start(bf16[2,12288]{1,0:T(2,128)(2,1)S(1)} %copy.74), channel_id=1, source_target_pairs={{0,1},{1,2},{2,3},{3,4},{4,5},{5,6},{6,7},{7,8},{8,9},{9,10},{10,1... | collective-permute-start | bytes 147464 | tf_op jit(solution)/shard_map/ppermute | solution.py:13
  39.4 4.1 %copy-start.18 = (f32[7,4096]{1,0:T(8,128)S(1)}, f32[7,4096]{1,0:T(8,128)}, u32[]{:S(2)}) copy-start(f32[7,4096]{1,0:T(8,128)} %param.10) | copy-start | bytes 344068
  41.5 7.4 %collective-permute-start.1 = (bf16[6,4096]{1,0:T(8,128)(2,1)S(1)}, bf16[6,4096]{1,0:T(8,128)(2,1)S(1)}, u32[]{:S(2)}, u32[]{:S(2)}) collective-permute-start(bf16[6,4096]{1,0:T(8,128)(2,1)S(1)} %bitcast.132), channel_id=1, source_target_pairs={{0,1},{1,2},{2,3},{3,4},{4,5},{5,6},{6,7},{7,8},{8,9},{9,10},{10,1... | collective-permute-start | bytes 147464 | tf_op jit(solution)/shard_map/ppermute | solution.py:13
  46.9 9.2 %copy-start.19 = (f32[4096]{0:T(1024)S(1)}, f32[4096]{0:T(1024)}, u32[]{:S(2)}) copy-start(f32[4096]{0:T(1024)} %param.11) | copy-start | bytes 49156
  56.1 3.6 copy-start.4
  56.1 2.3 copy-start.9
  59.7 1.6 copy-start.5
  61.3 29.1 %collective-permute-start.2 = (bf16[2,128,4096]{1,2,0:T(8,128)(2,1)S(1)}, bf16[2,128,4096]{1,2,0:T(8,128)(2,1)S(1)}, u32[]{:S(2)}, u32[]{:S(2)}) collective-permute-start(bf16[2,128,4096]{1,2,0:T(8,128)(2,1)S(1)} %bitcast.115), channel_id=1, source_target_pairs={{0,1},{1,2},{2,3},{3,4},{4,5},{5,6},{6,7},{7,8},{8,9},{9,10},{10,1... | collective-permute-start | bytes 6291464 | tf_op jit(solution)/shard_map/ppermute | solution.py:13
  90.4 1.3 copy-start.10
  91.8 29.1 %collective-permute-start.3 = (bf16[2,128,4096]{1,2,0:T(8,128)(2,1)S(1)}, bf16[2,128,4096]{1,2,0:T(8,128)(2,1)S(1)}, u32[]{:S(2)}, u32[]{:S(2)}) collective-permute-start(bf16[2,128,4096]{1,2,0:T(8,128)(2,1)S(1)} %collective-permute-done.2), channel_id=1, source_target_pairs={{0,1},{1,2},{2,3},{3,4},{4,5},{5,6},{6,7},{7,8},{8,9},{9,10},{10,1... | collective-permute-start | bytes 6291464 | tf_op jit(solution)/shard_map/ppermute | solution.py:13
  120.9 1.3 copy-start.12
  122.2 29.1 %collective-permute-start.4 = (bf16[2,128,4096]{1,2,0:T(8,128)(2,1)S(1)}, bf16[2,128,4096]{1,2,0:T(8,128)(2,1)S(1)}, u32[]{:S(2)}, u32[]{:S(2)}) collective-permute-start(bf16[2,128,4096]{1,2,0:T(8,128)(2,1)S(1)} %collective-permute-done.3), channel_id=1, source_target_pairs={{0,1},{1,2},{2,3},{3,4},{4,5},{5,6},{6,7},{7,8},{8,9},{9,10},{10,1... | collective-permute-start | bytes 6291464 | tf_op jit(solution)/shard_map/ppermute | solution.py:13
  151.4 1.3 copy-start.14
  152.7 29.2 %collective-permute-start.5 = (bf16[2,128,4096]{1,2,0:T(8,128)(2,1)S(1)}, bf16[2,128,4096]{1,2,0:T(8,128)(2,1)}, u32[]{:S(2)}, u32[]{:S(2)}) collective-permute-start(bf16[2,128,4096]{1,2,0:T(8,128)(2,1)S(1)} %collective-permute-done.4), channel_id=1, source_target_pairs={{0,1},{1,2},{2,3},{3,4},{4,5},{5,6},{6,7},{7,8},{8,9},{9,10},{10,1... | collective-permute-start | bytes 6291464 | tf_op jit(solution)/shard_map/ppermute | solution.py:13
  181.9 29.5 %collective-permute-start.6 = (bf16[2,128,4096]{1,2,0:T(8,128)(2,1)}, bf16[2,128,4096]{1,2,0:T(8,128)(2,1)}, u32[]{:S(2)}, u32[]{:S(2)}) collective-permute-start(bf16[2,128,4096]{1,2,0:T(8,128)(2,1)} %collective-permute-done.5), channel_id=1, source_target_pairs={{0,1},{1,2},{2,3},{3,4},{4,5},{5,6},{6,7},{7,8},{8,9},{9,10},{10,1... | collective-permute-start | bytes 6291464 | tf_op jit(solution)/shard_map/ppermute | solution.py:13
  184.0 29.3 %copy-start.11 = (bf16[2,128,4096]{1,2,0:T(8,128)(2,1)S(1)}, bf16[2,128,4096]{1,2,0:T(8,128)(2,1)}, u32[]{:S(2)}) copy-start(bf16[2,128,4096]{1,2,0:T(8,128)(2,1)} %copy-done.10) | copy-start | bytes 6291460
  184.4 29.2 %copy-start.13 = (bf16[2,128,4096]{1,2,0:T(8,128)(2,1)S(1)}, bf16[2,128,4096]{1,2,0:T(8,128)(2,1)}, u32[]{:S(2)}) copy-start(bf16[2,128,4096]{1,2,0:T(8,128)(2,1)} %copy-done.12) | copy-start | bytes 6291460
  211.4 29.3 %collective-permute-start.7 = (bf16[2,128,4096]{1,2,0:T(8,128)(2,1)}, bf16[2,128,4096]{1,2,0:T(8,128)(2,1)S(1)}, u32[]{:S(2)}, u32[]{:S(2)}) collective-permute-start(bf16[2,128,4096]{1,2,0:T(8,128)(2,1)} %collective-permute-done.6), channel_id=1, source_target_pairs={{0,1},{1,2},{2,3},{3,4},{4,5},{5,6},{6,7},{7,8},{8,9},{9,10},{10,1... | collective-permute-start | bytes 6291464 | tf_op jit(solution)/shard_map/ppermute | solution.py:13
  213.6 1.6 copy-start.15
  240.7 29.1 %collective-permute-start.8 = (bf16[2,128,4096]{1,2,0:T(8,128)(2,1)S(1)}, bf16[2,128,4096]{1,2,0:T(8,128)(2,1)S(1)}, u32[]{:S(2)}, u32[]{:S(2)}) collective-permute-start(bf16[2,128,4096]{1,2,0:T(8,128)(2,1)S(1)} %collective-permute-done.7), channel_id=1, source_target_pairs={{0,1},{1,2},{2,3},{3,4},{4,5},{5,6},{6,7},{7,8},{8,9},{9,10},{10,1... | collective-permute-start | bytes 6291464 | tf_op jit(solution)/shard_map/ppermute | solution.py:13
  304.9 5.5 %copy-start.6 = (bf16[3,128,32,128]{1,3,0,2:T(8,128)(2,1)S(1)}, bf16[3,128,32,128]{1,3,0,2:T(8,128)(2,1)}, u32[]{:S(2)}) copy-start(bf16[3,128,32,128]{1,3,0,2:T(8,128)(2,1)} %copy-done.5) | copy-start | bytes 9437188
  346.8 5.0 %copy-start.7 = (f32[8,128,1024]{2,1,0:T(8,128)S(1)}, f32[8,128,1024]{2,1,0:T(8,128)}, u32[]{:S(2)}) copy-start(f32[8,128,1024]{2,1,0:T(8,128)} %fusion.29) | copy-start | bytes 12582916
  346.8 5.0 %copy-start.8 = (f32[8,128,1024]{2,1,0:T(8,128)S(1)}, f32[8,128,1024]{2,1,0:T(8,128)}, u32[]{:S(2)}) copy-start(f32[8,128,1024]{2,1,0:T(8,128)} %fusion.31) | copy-start | bytes 12582916
  346.8 6.2 %copy-start.16 = (bf16[1024,8,128]{2,1,0:T(8,128)(2,1)S(1)}, bf16[1024,8,128]{2,1,0:T(8,128)(2,1)}, u32[]{:S(2)}) copy-start(bf16[1024,8,128]{2,1,0:T(8,128)(2,1)} %get-tuple-element.17) | copy-start | bytes 6291460
  346.8 11.8 %slice-start = ((s8[8388608]{0:T(1024)(128)(4,1)}), s8[4194304]{0:T(1024)(128)(4,1)S(1)}, s32[]{:S(2)}) async-start(s8[8388608]{0:T(1024)(128)(4,1)} %bitcast.113), calls=%async_computation | async-start | bytes 8388608
  353.0 5.7 %slice-start.1 = ((s8[8388608]{0:T(1024)(128)(4,1)}), s8[4194304]{0:T(1024)(128)(4,1)S(1)}, s32[]{:S(2)}) async-start(s8[8388608]{0:T(1024)(128)(4,1)} %bitcast.113), calls=%async_computation.1 | async-start | bytes 8388608
  371.0 6.1 %copy-start.1 = (bf16[32,128,384]{2,1,0:T(8,128)(2,1)S(1)}, bf16[32,128,384]{2,1,0:T(8,128)(2,1)}, u32[]{:S(2)}) copy-start(bf16[32,128,384]{2,1,0:T(8,128)(2,1)} %param.8) | copy-start | bytes 9437188
where the time goes:
time: 379 us; the launch traced here: 377 us
  waiting for transfers between devices  191 us (50%)
  local copies, waits for them, and re-layouts  113 us (30%)
  other arithmetic  28.1 us (7%)
  matrix products  27 us (7%)
  starting transfers between devices  17.4 us (5%)
    ppermute x9, waiting for transfers between devices, shifted_2(): return lax.ppermute(block, axis, route)  191 us
    unnamed x60, local copies, waits for them, and re-layouts  32.9 us
    slice x3, local copies, waits for them, and re-layouts, shards(): key_rows = window[:, 0].reshape(-1, head_count, head_dim)  25.3 us
    slice x2, local copies, waits for them, and re-layouts, shards(): value_rows = window[:, 1].reshape(-1, head_count, head_dim)  17.6 us
    ppermute x9, starting transfers between devices, shifted_2(): return lax.ppermute(block, axis, route)  17.4 us
    dot_general x4, matrix products, attend(): jnp.einsum('thd,lhd->htl', query_group, key_group, preferred_element_type...  16.1 us
    another operation x1, local copies, waits for them, and re-layouts, shards(): value_rows = window[:, 1].reshape(-1, head_count, head_dim)  13.4 us
    add x1, other arithmetic, causal_taps(): summed + jnp.where(allowed, shifted * filter_taps[shift_by][None, :], 0.0)  10 us
  transfers between devices with their start and end apart: 9, of which 9 were waited for; matrix products, arithmetic and copies ran while one was open for 2% of the time, Pallas kernels for 0%

commit v1 on v0

v1 whole, which is shorter than its diff:
```python
import functools

import jax
import jax.numpy as jnp
from jax import lax
from jax.experimental import pallas as pl
from jax.experimental.pallas import tpu as pltpu
from jax.sharding import PartitionSpec as P

GROUP = 8
HALO = 16
MESH = pl.DeviceIdType.MESH
F32 = jnp.float32
BF16 = jnp.bfloat16
NEG = -1e30


def remote(src, dst, send_sem, recv_sem, device):
    return pltpu.make_async_remote_copy(
        src_ref=src,
        dst_ref=dst,
        send_sem=send_sem,
        recv_sem=recv_sem,
        device_id={"ctx": device},
        device_id_type=MESH,
    )


def kernel(
    ctx,
    doc_ref,
    hid,
    in_w,
    feat_ref,
    inner_ref,
    gain_ref,
    attn_w,
    out,
    x_ext,
    w_in,
    w_attn,
    res_send,
    res_own,
    res_prev,
    sc_send,
    sc_own,
    sc_prev,
    ssq,
    q_own,
    k_own,
    v_own,
    k_prev,
    v_prev,
    acc_ref,
    m_ref,
    l_ref,
    out_buf,
    load_sem,
    halo_sem,
    next_send,
    own_send,
    own_recv,
    prev_recv,
    next_sc_send,
    own_sc_send,
    own_sc_recv,
    prev_sc_recv,
    out_send,
    out_recv,
    own_sem,
):
    tok, channels = hid.shape
    hd = w_in.shape[1]
    heads = w_in.shape[0]
    per = heads // GROUP
    wide = per * hd
    taps = feat_ref.shape[0]
    inner_taps = inner_ref.shape[0]
    me = lax.axis_index("ctx")
    r = lax.rem(me, GROUP)
    group = lax.div(me, GROUP)
    base = group * GROUP
    has_prev = group > 0
    has_next = group < ctx // GROUP - 1

    loads = [
        pltpu.make_async_copy(hid, x_ext.at[pl.ds(HALO, tok)], load_sem.at[0]),
        pltpu.make_async_copy(in_w, w_in, load_sem.at[1]),
    ]
    for s in range(3):
        loads.append(
            pltpu.make_async_copy(
                attn_w.at[s, pl.ds(r * per, per)],
                w_attn.at[:, :, pl.ds(s * hd, hd)],
                load_sem.at[2 + s],
            )
        )
    for copy in loads:
        copy.start()

    barrier = pltpu.get_barrier_semaphore()

    def signal_own(j, carry):
        @pl.when(j != r)
        def _():
            pl.semaphore_signal(
                barrier, inc=1, device_id={"ctx": base + j}, device_id_type=MESH
            )

        @pl.when(has_prev)
        def _():
            pl.semaphore_signal(
                barrier, inc=1, device_id={"ctx": base - GROUP + j}, device_id_type=MESH
            )

        return carry

    lax.fori_loop(0, GROUP, signal_own, 0)

    @pl.when(has_next)
    def _():
        pl.semaphore_wait(barrier, 2 * GROUP - 1)

    @pl.when(jnp.logical_not(has_next))
    def _():
        pl.semaphore_wait(barrier, GROUP - 1)

    halo = remote(
        hid.at[pl.ds(tok - HALO, HALO)],
        x_ext.at[pl.ds(0, HALO)],
        halo_sem.at[0],
        halo_sem.at[1],
        lax.rem(me + 1, ctx),
    )

    @pl.when(me < ctx - 1)
    def _():
        halo.start()

    def doc_step(d, carry):
        end = carry[0] + doc_ref[d]
        return (end,) + tuple(
            jnp.where(end <= block, end, begin)
            for begin, block in zip(carry[1:], [base + t for t in range(GROUP)] + [me])
        )

    zero = jnp.int32(0)
    found = lax.fori_loop(0, doc_ref.shape[0], doc_step, (zero,) * (GROUP + 2))
    begins = found[1 : GROUP + 1]
    my_begin = found[GROUP + 1]

    loads[0].wait()
    loads[1].wait()

    @pl.when(me > 0)
    def _():
        halo.wait_recv()

    @pl.when(me == 0)
    def _():
        x_ext[0:HALO, :] = jnp.zeros((HALO, channels), BF16)

    keep = jnp.where(my_begin < me, 1.0, 0.0).astype(F32)
    x_ext[0:HALO, :] = (x_ext[0:HALO, :].astype(F32) * keep).astype(BF16)

    ssq[...] = jnp.zeros_like(ssq)

    def mix_chunk(step, carry):
        chunk = lax.rem(r + 1 + step, GROUP)
        total = ssq[...]
        for hh in range(per):
            head = chunk * per + hh
            x = x_ext[:, pl.ds(pl.multiple_of(head * hd, hd), hd)]
            streams = jnp.dot(x, w_in[head], preferred_element_type=F32).astype(BF16).astype(F32)
            taps_f = feat_ref[:, pl.ds(pl.multiple_of(head * 3 * hd, 3 * hd), 3 * hd)]
            feats = streams * taps_f[0:1]
            for t in range(1, taps):
                feats = feats + pltpu.roll(streams, t, 0) * taps_f[t : t + 1]
            gated = (feats[:, hd : 2 * hd] * feats[:, 2 * hd :]).astype(BF16).astype(F32)
            taps_i = inner_ref[:, pl.ds(pl.multiple_of(head * hd, hd), hd)]
            conv = gated * taps_i[0:1]
            for t in range(1, inner_taps):
                conv = conv + pltpu.roll(gated, t, 0) * taps_i[t : t + 1]
            residual = (x[HALO:].astype(F32) + feats[HALO:, :hd] * conv[HALO:]).astype(BF16)
            res_send[chunk, :, hh * hd : (hh + 1) * hd] = residual
            res_float = residual.astype(F32)
            total = total + res_float * res_float
        ssq[...] = total

        @pl.when(has_next)
        def _():
            remote(
                res_send.at[chunk],
                res_prev.at[r],
                next_send.at[chunk],
                prev_recv.at[r],
                base + GROUP + chunk,
            ).start()

        @pl.when(chunk != r)
        def _():
            remote(
                res_send.at[chunk],
                res_own.at[r],
                own_send.at[chunk],
                own_recv.at[r],
                base + chunk,
            ).start()

        return carry

    lax.fori_loop(0, GROUP, mix_chunk, 0)
    keep_own = pltpu.make_async_copy(res_send.at[r], res_own.at[r], own_sem.at[0])
    keep_own.start()

    mean = jnp.sum(ssq[...], axis=-1, keepdims=True) * (1.0 / channels)
    scale = lax.rsqrt(mean + 1e-05)
    sc_send[...] = jnp.transpose(jnp.broadcast_to(scale, (tok, tok)))[0:8]

    def send_scale(j, carry):
        @pl.when(has_next)
        def _():
            remote(
                sc_send, sc_prev.at[r], next_sc_send.at[j], prev_sc_recv.at[r], base + GROUP + j
            ).start()

        @pl.when(j != r)
        def _():
            remote(sc_send, sc_own.at[r], own_sc_send.at[j], own_sc_recv.at[r], base + j).start()

        return carry

    lax.fori_loop(0, GROUP, send_scale, 0)
    sc_own[r] = sc_send[...]
    keep_own.wait()
    for copy in loads[2:]:
        copy.wait()
    gain = gain_ref[:, pl.ds(pl.multiple_of(r * wide, wide), wide)]

    def norm_head(res_tile, scales, hh):
        columns = slice(hh * hd, (hh + 1) * hd)
        return (res_tile[:, columns].astype(F32) * scales * gain[:, columns]).astype(BF16)

    def project_own(j, carry):
        @pl.when(j != r)
        def _():
            remote(res_send.at[j], res_own.at[j], own_send.at[j], own_recv.at[j], base + j).wait_recv()
            remote(sc_send, sc_own.at[j], own_sc_send.at[j], own_sc_recv.at[j], base + j).wait_recv()

        scales = jnp.transpose(jnp.broadcast_to(sc_own[j][0:1], (tok, tok)))
        tile = res_own[j]
        rows = pl.ds(pl.multiple_of(j * tok, tok), tok)
        for hh in range(per):
            normed = norm_head(tile, scales, hh)
            made = jnp.dot(normed, w_attn[hh], preferred_element_type=F32).astype(BF16)
            q_own[hh, rows, :] = made[:, :hd]
            k_own[hh, rows, :] = made[:, hd : 2 * hd]
            v_own[hh, rows, :] = made[:, 2 * hd :]
        return carry

    lax.fori_loop(0, GROUP, project_own, 0)

    slope = hd ** (-0.5)
    contract_last = (((1,), (1,)), ((), ()))

    def score(q, k):
        return lax.dot_general(q, k, contract_last, preferred_element_type=F32)

    def hidden_bias(first, count, begin_row):
        columns = first + lax.broadcasted_iota(jnp.int32, (1, count), 1)
        return jnp.where(columns >= begin_row, 0.0, NEG).astype(F32)

    def finish(hh, t, acc, total):
        columns = pl.ds(pl.multiple_of(hh * hd, hd), hd)
        res_float = res_own[t, :, columns].astype(F32)
        out_buf[t, :, columns] = (res_float + acc * (1.0 / total)).astype(BF16)

    def send_out(t):
        columns = pl.ds(pl.multiple_of(r * wide, wide), wide)

        @pl.when(r != t)
        def _():
            remote(
                out_buf.at[t], out.at[:, columns], out_send.at[t], out_recv.at[r], base + t
            ).start()

        @pl.when(r == t)
        def _():
            pltpu.make_async_copy(out_buf.at[t], out.at[:, columns], own_sem.at[1]).start()

    tri = lax.broadcasted_iota(jnp.int32, (tok, tok), 0) >= lax.broadcasted_iota(
        jnp.int32, (tok, tok), 1
    )

    for t in range(GROUP - 1, -1, -1):
        bias = hidden_bias(0, t * tok, (begins[t] - base) * tok) if t else None

        def own_head(hh, carry, t=t, bias=bias):
            q = q_own[hh, t * tok : (t + 1) * tok, :]
            diag = jnp.where(tri, score(q, k_own[hh, t * tok : (t + 1) * tok, :]), NEG)
            top = jnp.max(diag, axis=-1, keepdims=True)
            if t:
                bulk = score(q, k_own[hh, : t * tok, :]) + bias
                top = jnp.maximum(top, jnp.max(bulk, axis=-1, keepdims=True))
            exps = jnp.exp((diag - top) * slope)
            total = jnp.sum(exps, axis=-1, keepdims=True)
            acc = jnp.dot(
                exps.astype(BF16), v_own[hh, t * tok : (t + 1) * tok, :], preferred_element_type=F32
            )
            if t:
                exps = jnp.exp((bulk - top) * slope)
                total = total + jnp.sum(exps, axis=-1, keepdims=True)
                acc = acc + jnp.dot(
                    exps.astype(BF16), v_own[hh, : t * tok, :], preferred_element_type=F32
                )
            if t == GROUP - 1:
                finish(hh, t, acc, total)
            else:
                acc_ref[hh, t] = acc
                m_ref[hh, t] = jnp.broadcast_to(top, (tok, hd))
                l_ref[hh, t] = jnp.broadcast_to(total, (tok, hd))
            return carry

        lax.fori_loop(0, per, own_head, 0)
        if t == GROUP - 1:
            send_out(t)

    def project_prev(j, carry):
        @pl.when(has_prev)
        def _():
            remote(res_send.at[j], res_prev.at[j], next_send.at[j], prev_recv.at[j], base + j).wait_recv()
            remote(sc_send, sc_prev.at[j], next_sc_send.at[j], prev_sc_recv.at[j], base + j).wait_recv()
            scales = jnp.transpose(jnp.broadcast_to(sc_prev[j][0:1], (tok, tok)))
            tile = res_prev[j]
            rows = pl.ds(pl.multiple_of(j * tok, tok), tok)
            for hh in range(per):
                normed = norm_head(tile, scales, hh)
                made = jnp.dot(normed, w_attn[hh][:, hd:], preferred_element_type=F32).astype(BF16)
                k_prev[hh, rows, :] = made[:, :hd]
                v_prev[hh, rows, :] = made[:, hd:]

        @pl.when(jnp.logical_not(has_prev))
        def _():
            rows = pl.ds(pl.multiple_of(j * tok, tok), tok)
            for hh in range(per):
                k_prev[hh, rows, :] = jnp.zeros((tok, hd), BF16)
                v_prev[hh, rows, :] = jnp.zeros((tok, hd), BF16)

        return carry

    lax.fori_loop(0, GROUP, project_prev, 0)

    for t in range(GROUP - 2, -1, -1):
        first = (t + 1) * tok
        count = (GROUP - 1 - t) * tok
        bias = hidden_bias(first, count, (begins[t] - base + GROUP) * tok)

        def prev_head(hh, carry, t=t, first=first, bias=bias):
            q = q_own[hh, t * tok : (t + 1) * tok, :]
            bulk = score(q, k_prev[hh, first:, :]) + bias
            before = m_ref[hh, t][:, 0:1]
            top = jnp.maximum(before, jnp.max(bulk, axis=-1, keepdims=True))
            exps = jnp.exp((bulk - top) * slope)
            fade = jnp.exp((before - top) * slope)
            total = l_ref[hh, t][:, 0:1] * fade + jnp.sum(exps, axis=-1, keepdims=True)
            acc = acc_ref[hh, t] * fade + jnp.dot(
                exps.astype(BF16), v_prev[hh, first:, :], preferred_element_type=F32
            )
            finish(hh, t, acc, total)
            return carry

        lax.fori_loop(0, per, prev_head, 0)
        send_out(t)

    @pl.when(me < ctx - 1)
    def _():
        halo.wait_send()

    def drain(j, carry):
        @pl.when(has_next)
        def _():
            remote(res_send.at[j], res_prev.at[r], next_send.at[j], prev_recv.at[r], base + j).wait_send()
            remote(sc_send, sc_prev.at[r], next_sc_send.at[j], prev_sc_recv.at[r], base + j).wait_send()

        @pl.when(j != r)
        def _():
            remote(res_send.at[j], res_own.at[r], own_send.at[j], own_recv.at[r], base + j).wait_send()
            remote(sc_send, sc_own.at[r], own_sc_send.at[j], own_sc_recv.at[r], base + j).wait_send()
            columns = pl.ds(pl.multiple_of(j * wide, wide), wide)
            sent = remote(out_buf.at[j], out.at[:, columns], out_send.at[j], out_recv.at[j], base + j)
            sent.wait_send()
            sent.wait_recv()

        @pl.when(j == r)
        def _():
            columns = pl.ds(pl.multiple_of(r * wide, wide), wide)
            pltpu.make_async_copy(out_buf.at[j], out.at[:, columns], own_sem.at[1]).wait()

        return carry

    lax.fori_loop(0, GROUP, drain, 0)


def shards(ctx, hidden_in, in_weight, feat_filter, inner_filter, norm_gain, attn_weight, doc_lengths):
    tok, channels = hidden_in.shape
    heads, hd, _ = in_weight.shape
    per = heads // GROUP
    wide = per * hd
    span = GROUP * tok
    any_spec = pl.BlockSpec(memory_space=pl.ANY)
    vmem_spec = pl.BlockSpec(memory_space=pltpu.VMEM)
    dma = pltpu.SemaphoreType.DMA
    return pl.pallas_call(
        functools.partial(kernel, ctx),
        out_shape=jax.ShapeDtypeStruct((tok, channels), BF16),
        in_specs=[
            pl.BlockSpec(memory_space=pltpu.SMEM),
            any_spec,
            any_spec,
            vmem_spec,
            vmem_spec,
            vmem_spec,
            any_spec,
        ],
        out_specs=any_spec,
        scratch_shapes=[
            pltpu.VMEM((HALO + tok, channels), BF16),
            pltpu.VMEM((heads, hd, 3 * hd), BF16),
            pltpu.VMEM((per, hd, 3 * hd), BF16),
            pltpu.VMEM((GROUP, tok, wide), BF16),
            pltpu.VMEM((GROUP, tok, wide), BF16),
            pltpu.VMEM((GROUP, tok, wide), BF16),
            pltpu.VMEM((8, tok), F32),
            pltpu.VMEM((GROUP, 8, tok), F32),
            pltpu.VMEM((GROUP, 8, tok), F32),
            pltpu.VMEM((tok, hd), F32),
            pltpu.VMEM((per, span, hd), BF16),
            pltpu.VMEM((per, span, hd), BF16),
            pltpu.VMEM((per, span, hd), BF16),
            pltpu.VMEM((per, span, hd), BF16),
            pltpu.VMEM((per, span, hd), BF16),
            pltpu.VMEM((per, GROUP, tok, hd), F32),
            pltpu.VMEM((per, GROUP, tok, hd), F32),
            pltpu.VMEM((per, GROUP, tok, hd), F32),
            pltpu.VMEM((GROUP, tok, wide), BF16),
            dma((5,)),
            dma((2,)),
        ]
        + [dma((GROUP,))] * 10
        + [dma((2,))],
        compiler_params=pltpu.CompilerParams(
            collective_id=0, has_side_effects=True, vmem_limit_bytes=56 * 1024 * 1024
        ),
        cost_estimate=pl.CostEstimate(
            flops=6_000_000_000, bytes_accessed=9_000_000, transcendentals=4_200_000
        ),
    )(
        doc_lengths,
        hidden_in,
        in_weight,
        feat_filter,
        inner_filter,
        norm_gain.reshape(1, channels),
        attn_weight,
    )


def solution(mesh):
    return jax.shard_map(
        functools.partial(shards, mesh.shape["ctx"]),
        mesh=mesh,
        in_specs=(P(("groups", "ctx"), None), P(), P(), P(), P(), P(), P("groups")),
        out_specs=P(("groups", "ctx"), None),
        check_vma=False,
    )
```

time: 379 us -> 82.1 us (0.22)
  the two profiles are of different devices: /device:TPU:24 before, /device:TPU:16 now
where the time goes in v1:
time: 82.1 us; the launch traced here: 81.9 us
  Pallas kernels  79.6 us (97%)
  local copies, waits for them, and re-layouts  2.29 us (3%)
    pallas_call x1, Pallas kernels, shards(): pl.pallas_call(functools.partial(kernel, ctx), out_shape=jax.ShapeDtypeSt...  79.6 us
    unnamed x1, local copies, waits for them, and re-layouts  2.29 us

profile of v1, /device:TPU:16, one launch (start us, length us, event | category | flops | bytes accessed | tf_op | source)
XLA Modules:
  0.0 81.9 jit_solution(17422025531944246944)
XLA Ops:
  0.0 79.6 %shard_map.73 = bf16[128,4096]{1,0:T(8,128)(2,1)} custom-call(s32[8]{0:T(128)} %doc_ref.1, bf16[128,4096]{1,0:T(8,128)(2,1)} %hid.1, bf16[32,128,384]{2,1,0:T(8,128)(2,1)} %in_w.1, f32[3,12288]{1,0:T(4,128)} %feat_ref.1, f32[7,4096]{1,0:T(8,128)} %inner_ref.1, f32[1,4096]{1,0:T(1,128)} %bitcast.1, bf16[3,32,128,128]{3,2,1,0:T(8,128)(2,1)} %attn_w.1), custom_call_target="tpu_custom_call" | custom-call | flops 6000000000 | bytes 9000000 | tf_op jit(solution)/shard_map/pallas_call | solution.py:413
  79.6 2.3 %copy.9 = bf16[128,4096]{1,0:T(8,128)(2,1)} copy(bf16[128,4096]{1,0:T(8,128)(2,1)} %shard_map.73) | data formatting | bytes 2097152

commit v2 on v1

--- a/solution.py
+++ b/solution.py
@@ -9,6 +9,7 @@
 
 GROUP = 8
 HALO = 16
+LAG = 3
 MESH = pl.DeviceIdType.MESH
 F32 = jnp.float32
 BF16 = jnp.bfloat16
@@ -107,23 +108,20 @@
                 barrier, inc=1, device_id={"ctx": base + j}, device_id_type=MESH
             )
 
-        @pl.when(has_prev)
-        def _():
-            pl.semaphore_signal(
-                barrier, inc=1, device_id={"ctx": base - GROUP + j}, device_id_type=MESH
-            )
-
         return carry
 
     lax.fori_loop(0, GROUP, signal_own, 0)
 
-    @pl.when(has_next)
-    def _():
-        pl.semaphore_wait(barrier, 2 * GROUP - 1)
-
-    @pl.when(jnp.logical_not(has_next))
-    def _():
-        pl.semaphore_wait(barrier, GROUP - 1)
+    @pl.when(has_prev)
+    def _():
+        pl.semaphore_signal(barrier, inc=1, device_id={"ctx": me - GROUP}, device_id_type=MESH)
+
+    @pl.when(has_prev & (r == 0))
+    def _():
+        pl.semaphore_signal(barrier, inc=1, device_id={"ctx": me - 1}, device_id_type=MESH)
+
+    hears = jnp.where(has_next, jnp.where(r == GROUP - 1, GROUP + 1, GROUP), GROUP - 1)
+    pl.semaphore_wait(barrier, hears)
 
     halo = remote(
         hid.at[pl.ds(tok - HALO, HALO)],
@@ -164,6 +162,18 @@
     x_ext[0:HALO, :] = (x_ext[0:HALO, :].astype(F32) * keep).astype(BF16)
 
     ssq[...] = jnp.zeros_like(ssq)
+
+    def forward(j, src):
+        @pl.when(has_next & (j > 0))
+        def _():
+            remote(
+                src, res_prev.at[j], next_send.at[j], prev_recv.at[j], me + GROUP
+            ).start()
+
+    def receive_own(step):
+        j = lax.rem(r + 2 * GROUP - 1 - step, GROUP)
+        remote(res_send.at[j], res_own.at[j], own_send.at[j], own_recv.at[j], base + j).wait_recv()
+        forward(j, res_own.at[j])
 
     def mix_chunk(step, carry):
         chunk = lax.rem(r + 1 + step, GROUP)
@@ -187,16 +197,6 @@
             total = total + res_float * res_float
         ssq[...] = total
 
-        @pl.when(has_next)
-        def _():
-            remote(
-                res_send.at[chunk],
-                res_prev.at[r],
-                next_send.at[chunk],
-                prev_recv.at[r],
-                base + GROUP + chunk,
-            ).start()
-
         @pl.when(chunk != r)
         def _():
             remote(
@@ -207,23 +207,22 @@
                 base + chunk,
             ).start()
 
+        @pl.when(step >= LAG)
+        def _():
+            receive_own(step - LAG)
+
         return carry
 
     lax.fori_loop(0, GROUP, mix_chunk, 0)
     keep_own = pltpu.make_async_copy(res_send.at[r], res_own.at[r], own_sem.at[0])
     keep_own.start()
+    forward(r, res_send.at[r])
 
     mean = jnp.sum(ssq[...], axis=-1, keepdims=True) * (1.0 / channels)
     scale = lax.rsqrt(mean + 1e-05)
     sc_send[...] = jnp.transpose(jnp.broadcast_to(scale, (tok, tok)))[0:8]
 
     def send_scale(j, carry):
-        @pl.when(has_next)
-        def _():
-            remote(
-                sc_send, sc_prev.at[r], next_sc_send.at[j], prev_sc_recv.at[r], base + GROUP + j
-            ).start()
-
         @pl.when(j != r)
         def _():
             remote(sc_send, sc_own.at[r], own_sc_send.at[j], own_sc_recv.at[r], base + j).start()
@@ -232,6 +231,25 @@
 
     lax.fori_loop(0, GROUP, send_scale, 0)
     sc_own[r] = sc_send[...]
+    for step in range(GROUP - LAG, GROUP - 1):
+        receive_own(step)
+
+    def receive_scale(j, carry):
+        @pl.when(j != r)
+        def _():
+            remote(sc_send, sc_own.at[j], own_sc_send.at[j], own_sc_recv.at[j], base + j).wait_recv()
+
+        return carry
+
+    lax.fori_loop(0, GROUP, receive_scale, 0)
+    scales_on = remote(
+        sc_own, sc_prev, next_sc_send.at[0], prev_sc_recv.at[0], lax.rem(me + GROUP, ctx)
+    )
+
+    @pl.when(has_next)
+    def _():
+        scales_on.start()
+
     keep_own.wait()
     for copy in loads[2:]:
         copy.wait()
@@ -242,11 +260,6 @@
         return (res_tile[:, columns].astype(F32) * scales * gain[:, columns]).astype(BF16)
 
     def project_own(j, carry):
-        @pl.when(j != r)
-        def _():
-            remote(res_send.at[j], res_own.at[j], own_send.at[j], own_recv.at[j], base + j).wait_recv()
-            remote(sc_send, sc_own.at[j], own_sc_send.at[j], own_sc_recv.at[j], base + j).wait_recv()
-
         scales = jnp.transpose(jnp.broadcast_to(sc_own[j][0:1], (tok, tok)))
         tile = res_own[j]
         rows = pl.ds(pl.multiple_of(j * tok, tok), tok)
@@ -328,8 +341,7 @@
     def project_prev(j, carry):
         @pl.when(has_prev)
         def _():
-            remote(res_send.at[j], res_prev.at[j], next_send.at[j], prev_recv.at[j], base + j).wait_recv()
-            remote(sc_send, sc_prev.at[j], next_sc_send.at[j], prev_sc_recv.at[j], base + j).wait_recv()
+            remote(res_own.at[j], res_prev.at[j], next_send.at[j], prev_recv.at[j], me).wait_recv()
             scales = jnp.transpose(jnp.broadcast_to(sc_prev[j][0:1], (tok, tok)))
             tile = res_prev[j]
             rows = pl.ds(pl.multiple_of(j * tok, tok), tok)
@@ -348,9 +360,13 @@
 
         return carry
 
-    lax.fori_loop(0, GROUP, project_prev, 0)
-
-    for t in range(GROUP - 2, -1, -1):
+    @pl.when(has_prev)
+    def _():
+        scales_on.wait_recv()
+
+    lax.fori_loop(1, GROUP, project_prev, 0)
+
+    def attend_prev(t):
         first = (t + 1) * tok
         count = (GROUP - 1 - t) * tok
         bias = hidden_bias(first, count, (begins[t] - base + GROUP) * tok)
@@ -370,17 +386,32 @@
             return carry
 
         lax.fori_loop(0, per, prev_head, 0)
-        send_out(t)
+
+    def attend_step(step, carry):
+        tile = lax.rem(r + 1 + step, GROUP)
+        for t in range(GROUP - 1):
+            pl.when(tile == t)(functools.partial(attend_prev, t))
+
+        @pl.when(tile < GROUP - 1)
+        def _():
+            send_out(tile)
+
+        return carry
+
+    lax.fori_loop(0, GROUP, attend_step, 0)
 
     @pl.when(me < ctx - 1)
     def _():
         halo.wait_send()
 
+    @pl.when(has_next)
+    def _():
+        scales_on.wait_send()
+
     def drain(j, carry):
-        @pl.when(has_next)
-        def _():
-            remote(res_send.at[j], res_prev.at[r], next_send.at[j], prev_recv.at[r], base + j).wait_send()
-            remote(sc_send, sc_prev.at[r], next_sc_send.at[j], prev_sc_recv.at[r], base + j).wait_send()
+        @pl.when(has_next & (j > 0))
+        def _():
+            remote(res_own.at[j], res_prev.at[j], next_send.at[j], prev_recv.at[j], me).wait_send()
 
         @pl.when(j != r)
         def _():

time: 82.1 us -> 66.3 us (0.81)
  the two profiles are of different devices: /device:TPU:16 before, /device:TPU:19 now
where the time goes in v2:
time: 66.3 us; the launch traced here: 66.2 us
  Pallas kernels  63.9 us (96%)
  local copies, waits for them, and re-layouts  2.29 us (3%)
    pallas_call x1, Pallas kernels, shards(): pl.pallas_call(functools.partial(kernel, ctx), out_shape=jax.ShapeDtypeSt...  63.9 us
    unnamed x1, local copies, waits for them, and re-layouts  2.29 us

profile of v2, /device:TPU:19, one launch (start us, length us, event | category | flops | bytes accessed | tf_op | source)
XLA Modules:
  0.0 66.2 jit_solution(13712472192811497266)
XLA Ops:
  0.0 63.9 %shard_map.73 = bf16[128,4096]{1,0:T(8,128)(2,1)} custom-call(s32[8]{0:T(128)} %doc_ref.1, bf16[128,4096]{1,0:T(8,128)(2,1)} %hid.1, bf16[32,128,384]{2,1,0:T(8,128)(2,1)} %in_w.1, f32[3,12288]{1,0:T(4,128)} %feat_ref.1, f32[7,4096]{1,0:T(8,128)} %inner_ref.1, f32[1,4096]{1,0:T(1,128)} %bitcast.1, bf16[3,32,128,128]{3,2,1,0:T(8,128)(2,1)} %attn_w.1), custom_call_target="tpu_custom_call" | custom-call | flops 6000000000 | bytes 9000000 | tf_op jit(solution)/shard_map/pallas_call | solution.py:444
  63.9 2.3 %copy.9 = bf16[128,4096]{1,0:T(8,128)(2,1)} copy(bf16[128,4096]{1,0:T(8,128)(2,1)} %shard_map.73) | data formatting | bytes 2097152

commit v3 on v2

--- a/solution.py
+++ b/solution.py
@@ -14,6 +14,7 @@
 F32 = jnp.float32
 BF16 = jnp.bfloat16
 NEG = -1e30
+LOG2_E = 1.4426950408889634
 
 
 def remote(src, dst, send_sem, recv_sem, device):
@@ -32,12 +33,15 @@
     doc_ref,
     hid,
     in_w,
+    feat_hbm,
+    inner_hbm,
+    gain_hbm,
+    attn_w,
+    out,
+    x_ext,
     feat_ref,
     inner_ref,
     gain_ref,
-    attn_w,
-    out,
-    x_ext,
     w_in,
     w_attn,
     res_send,
@@ -52,9 +56,6 @@
     v_own,
     k_prev,
     v_prev,
-    acc_ref,
-    m_ref,
-    l_ref,
     out_buf,
     load_sem,
     halo_sem,
@@ -96,6 +97,11 @@
                 load_sem.at[2 + s],
             )
         )
+    loads += [
+        pltpu.make_async_copy(feat_hbm, feat_ref, load_sem.at[5]),
+        pltpu.make_async_copy(inner_hbm, inner_ref, load_sem.at[6]),
+        pltpu.make_async_copy(gain_hbm, gain_ref, load_sem.at[7]),
+    ]
     for copy in loads:
         copy.start()
 
@@ -149,6 +155,8 @@
 
     loads[0].wait()
     loads[1].wait()
+    loads[5].wait()
+    loads[6].wait()
 
     @pl.when(me > 0)
     def _():
@@ -251,7 +259,7 @@
         scales_on.start()
 
     keep_own.wait()
-    for copy in loads[2:]:
+    for copy in loads[2:5] + loads[7:]:
         copy.wait()
     gain = gain_ref[:, pl.ds(pl.multiple_of(r * wide, wide), wide)]
 
@@ -273,7 +281,7 @@
 
     lax.fori_loop(0, GROUP, project_own, 0)
 
-    slope = hd ** (-0.5)
+    slope = hd ** (-0.5) * LOG2_E
     contract_last = (((1,), (1,)), ((), ()))
 
     def score(q, k):
@@ -304,39 +312,6 @@
     tri = lax.broadcasted_iota(jnp.int32, (tok, tok), 0) >= lax.broadcasted_iota(
         jnp.int32, (tok, tok), 1
     )
-
-    for t in range(GROUP - 1, -1, -1):
-        bias = hidden_bias(0, t * tok, (begins[t] - base) * tok) if t else None
-
-        def own_head(hh, carry, t=t, bias=bias):
-            q = q_own[hh, t * tok : (t + 1) * tok, :]
-            diag = jnp.where(tri, score(q, k_own[hh, t * tok : (t + 1) * tok, :]), NEG)
-            top = jnp.max(diag, axis=-1, keepdims=True)
-            if t:
-                bulk = score(q, k_own[hh, : t * tok, :]) + bias
-                top = jnp.maximum(top, jnp.max(bulk, axis=-1, keepdims=True))
-            exps = jnp.exp((diag - top) * slope)
-            total = jnp.sum(exps, axis=-1, keepdims=True)
-            acc = jnp.dot(
-                exps.astype(BF16), v_own[hh, t * tok : (t + 1) * tok, :], preferred_element_type=F32
-            )
-            if t:
-                exps = jnp.exp((bulk - top) * slope)
-                total = total + jnp.sum(exps, axis=-1, keepdims=True)
-                acc = acc + jnp.dot(
-                    exps.astype(BF16), v_own[hh, : t * tok, :], preferred_element_type=F32
-                )
-            if t == GROUP - 1:
-                finish(hh, t, acc, total)
-            else:
-                acc_ref[hh, t] = acc
-                m_ref[hh, t] = jnp.broadcast_to(top, (tok, hd))
-                l_ref[hh, t] = jnp.broadcast_to(total, (tok, hd))
-            return carry
-
-        lax.fori_loop(0, per, own_head, 0)
-        if t == GROUP - 1:
-            send_out(t)
 
     def project_prev(j, carry):
         @pl.when(has_prev)
@@ -366,36 +341,42 @@
 
     lax.fori_loop(1, GROUP, project_prev, 0)
 
-    def attend_prev(t):
+    def attend(t):
+        own = slice(t * tok, (t + 1) * tok)
         first = (t + 1) * tok
-        count = (GROUP - 1 - t) * tok
-        bias = hidden_bias(first, count, (begins[t] - base + GROUP) * tok)
-
-        def prev_head(hh, carry, t=t, first=first, bias=bias):
-            q = q_own[hh, t * tok : (t + 1) * tok, :]
-            bulk = score(q, k_prev[hh, first:, :]) + bias
-            before = m_ref[hh, t][:, 0:1]
-            top = jnp.maximum(before, jnp.max(bulk, axis=-1, keepdims=True))
-            exps = jnp.exp((bulk - top) * slope)
-            fade = jnp.exp((before - top) * slope)
-            total = l_ref[hh, t][:, 0:1] * fade + jnp.sum(exps, axis=-1, keepdims=True)
-            acc = acc_ref[hh, t] * fade + jnp.dot(
-                exps.astype(BF16), v_prev[hh, first:, :], preferred_element_type=F32
+        bias_own = hidden_bias(0, t * tok, (begins[t] - base) * tok) if t else None
+        bias_prev = (
+            hidden_bias(first, (GROUP - 1 - t) * tok, (begins[t] - base + GROUP) * tok)
+            if t < GROUP - 1
+            else None
+        )
+
+        def one_head(hh, carry):
+            q = q_own[hh, own, :]
+            parts = [(jnp.where(tri, score(q, k_own[hh, own, :]), NEG), v_own[hh, own, :])]
+            if t:
+                parts.append((score(q, k_own[hh, : t * tok, :]) + bias_own, v_own[hh, : t * tok, :]))
+            if t < GROUP - 1:
+                parts.append((score(q, k_prev[hh, first:, :]) + bias_prev, v_prev[hh, first:, :]))
+            top = functools.reduce(
+                jnp.maximum, [jnp.max(part, axis=-1, keepdims=True) for part, _ in parts]
             )
+            total = 0.0
+            acc = 0.0
+            for part, values in parts:
+                exps = jnp.exp2((part - top) * slope)
+                total = total + jnp.sum(exps, axis=-1, keepdims=True)
+                acc = acc + jnp.dot(exps.astype(BF16), values, preferred_element_type=F32)
             finish(hh, t, acc, total)
             return carry
 
-        lax.fori_loop(0, per, prev_head, 0)
+        lax.fori_loop(0, per, one_head, 0, unroll=True)
 
     def attend_step(step, carry):
         tile = lax.rem(r + 1 + step, GROUP)
-        for t in range(GROUP - 1):
-            pl.when(tile == t)(functools.partial(attend_prev, t))
-
-        @pl.when(tile < GROUP - 1)
-        def _():
-            send_out(tile)
-
+        for t in range(GROUP):
+            pl.when(tile == t)(functools.partial(attend, t))
+        send_out(tile)
         return carry
 
     lax.fori_loop(0, GROUP, attend_step, 0)
@@ -439,7 +420,6 @@
     wide = per * hd
     span = GROUP * tok
     any_spec = pl.BlockSpec(memory_space=pl.ANY)
-    vmem_spec = pl.BlockSpec(memory_space=pltpu.VMEM)
     dma = pltpu.SemaphoreType.DMA
     return pl.pallas_call(
         functools.partial(kernel, ctx),
@@ -448,14 +428,17 @@
             pl.BlockSpec(memory_space=pltpu.SMEM),
             any_spec,
             any_spec,
-            vmem_spec,
-            vmem_spec,
-            vmem_spec,
+            any_spec,
+            any_spec,
+            any_spec,
             any_spec,
         ],
         out_specs=any_spec,
         scratch_shapes=[
             pltpu.VMEM((HALO + tok, channels), BF16),
+            pltpu.VMEM(feat_filter.shape, F32),
+            pltpu.VMEM(inner_filter.shape, F32),
+            pltpu.VMEM((1, channels), F32),
             pltpu.VMEM((heads, hd, 3 * hd), BF16),
             pltpu.VMEM((per, hd, 3 * hd), BF16),
             pltpu.VMEM((GROUP, tok, wide), BF16),
@@ -470,11 +453,8 @@
             pltpu.VMEM((per, span, hd), BF16),
             pltpu.VMEM((per, span, hd), BF16),
             pltpu.VMEM((per, span, hd), BF16),
-            pltpu.VMEM((per, GROUP, tok, hd), F32),
-            pltpu.VMEM((per, GROUP, tok, hd), F32),
-            pltpu.VMEM((per, GROUP, tok, hd), F32),
             pltpu.VMEM((GROUP, tok, wide), BF16),
-            dma((5,)),
+            dma((8,)),
             dma((2,)),
         ]
         + [dma((GROUP,))] * 10

time: 66.3 us -> 55 us (0.83)
  Pallas kernels: 63.9 us -> 52.2 us
    pallas_call x1, Pallas kernels: 63.9 us -> 52.2 us  [shards(): pl.pallas_call(functools.partial(kernel, ctx), out_shape=jax.ShapeDtypeSt...]
where the time goes in v3:
time: 55 us; the launch traced here: 54.5 us
  Pallas kernels  52.2 us (95%)
  local copies, waits for them, and re-layouts  2.29 us (4%)
    pallas_call x1, Pallas kernels, shards(): pl.pallas_call(functools.partial(kernel, ctx), out_shape=jax.ShapeDtypeSt...  52.2 us
    unnamed x1, local copies, waits for them, and re-layouts  2.29 us

profile of v3, /device:TPU:19, one launch (start us, length us, event | category | flops | bytes accessed | tf_op | source)
XLA Modules:
  0.0 54.5 jit_solution(6310686748888084970)
XLA Ops:
  0.0 52.2 %shard_map.73 = bf16[128,4096]{1,0:T(8,128)(2,1)} custom-call(s32[8]{0:T(128)} %doc_ref.1, bf16[128,4096]{1,0:T(8,128)(2,1)} %hid.1, bf16[32,128,384]{2,1,0:T(8,128)(2,1)} %in_w.1, f32[3,12288]{1,0:T(4,128)} %feat_hbm.1, f32[7,4096]{1,0:T(8,128)} %inner_hbm.1, f32[1,4096]{1,0:T(1,128)} %bitcast.1, bf16[3,32,128,128]{3,2,1,0:T(8,128)(2,1)} %attn_w.1), custom_call_target="tpu_custom_call" | custom-call | flops 6000000000 | bytes 9000000 | tf_op jit(solution)/shard_map/pallas_call | solution.py:424
  52.2 2.3 %copy.9 = bf16[128,4096]{1,0:T(8,128)(2,1)} copy(bf16[128,4096]{1,0:T(8,128)(2,1)} %shard_map.73) | data formatting | bytes 2097152

commit v4 on v3

--- a/solution.py
+++ b/solution.py
@@ -279,7 +279,7 @@
             v_own[hh, rows, :] = made[:, 2 * hd :]
         return carry
 
-    lax.fori_loop(0, GROUP, project_own, 0)
+    lax.fori_loop(0, GROUP, project_own, 0, unroll=4)
 
     slope = hd ** (-0.5) * LOG2_E
     contract_last = (((1,), (1,)), ((), ()))
@@ -312,34 +312,6 @@
     tri = lax.broadcasted_iota(jnp.int32, (tok, tok), 0) >= lax.broadcasted_iota(
         jnp.int32, (tok, tok), 1
     )
-
-    def project_prev(j, carry):
-        @pl.when(has_prev)
-        def _():
-            remote(res_own.at[j], res_prev.at[j], next_send.at[j], prev_recv.at[j], me).wait_recv()
-            scales = jnp.transpose(jnp.broadcast_to(sc_prev[j][0:1], (tok, tok)))
-            tile = res_prev[j]
-            rows = pl.ds(pl.multiple_of(j * tok, tok), tok)
-            for hh in range(per):
-                normed = norm_head(tile, scales, hh)
-                made = jnp.dot(normed, w_attn[hh][:, hd:], preferred_element_type=F32).astype(BF16)
-                k_prev[hh, rows, :] = made[:, :hd]
-                v_prev[hh, rows, :] = made[:, hd:]
-
-        @pl.when(jnp.logical_not(has_prev))
-        def _():
-            rows = pl.ds(pl.multiple_of(j * tok, tok), tok)
-            for hh in range(per):
-                k_prev[hh, rows, :] = jnp.zeros((tok, hd), BF16)
-                v_prev[hh, rows, :] = jnp.zeros((tok, hd), BF16)
-
-        return carry
-
-    @pl.when(has_prev)
-    def _():
-        scales_on.wait_recv()
-
-    lax.fori_loop(1, GROUP, project_prev, 0)
 
     def attend(t):
         own = slice(t * tok, (t + 1) * tok)
@@ -372,11 +344,44 @@
 
         lax.fori_loop(0, per, one_head, 0, unroll=True)
 
+    attend(GROUP - 1)
+    send_out(GROUP - 1)
+
+    def take_prev(j):
+        remote(res_own.at[j], res_prev.at[j], next_send.at[j], prev_recv.at[j], me).wait_recv()
+
+    def project_prev(j):
+        scales = jnp.transpose(jnp.broadcast_to(sc_prev[j][0:1], (tok, tok)))
+        tile = res_prev[j]
+        rows = slice(j * tok, (j + 1) * tok)
+        for hh in range(per):
+            normed = norm_head(tile, scales, hh)
+            made = jnp.dot(normed, w_attn[hh][:, hd:], preferred_element_type=F32).astype(BF16)
+            k_prev[hh, rows, :] = made[:, :hd]
+            v_prev[hh, rows, :] = made[:, hd:]
+
+    @pl.when(has_prev)
+    def _():
+        scales_on.wait_recv()
+        for j in range(1, GROUP):
+            take_prev(j)
+        for j in range(1, GROUP):
+            project_prev(j)
+
+    @pl.when(jnp.logical_not(has_prev))
+    def _():
+        k_prev[...] = jnp.zeros_like(k_prev)
+        v_prev[...] = jnp.zeros_like(v_prev)
+
     def attend_step(step, carry):
         tile = lax.rem(r + 1 + step, GROUP)
-        for t in range(GROUP):
+        for t in range(GROUP - 1):
             pl.when(tile == t)(functools.partial(attend, t))
-        send_out(tile)
+
+        @pl.when(tile < GROUP - 1)
+        def _():
+            send_out(tile)
+
         return carry
 
     lax.fori_loop(0, GROUP, attend_step, 0)

time: 55 us -> 53.3 us (0.969)
  Pallas kernels: 52.2 us -> 50.8 us
    pallas_call x1, Pallas kernels: 52.2 us -> 50.8 us  [shards(): pl.pallas_call(functools.partial(kernel, ctx), out_shape=jax.ShapeDtypeSt...]
where the time goes in v4:
time: 53.3 us; the launch traced here: 53.1 us
  Pallas kernels  50.8 us (95%)
  local copies, waits for them, and re-layouts  2.29 us (4%)
    pallas_call x1, Pallas kernels, shards(): pl.pallas_call(functools.partial(kernel, ctx), out_shape=jax.ShapeDtypeSt...  50.8 us
    unnamed x1, local copies, waits for them, and re-layouts  2.29 us

profile of v4, /device:TPU:19, one launch (start us, length us, event | category | flops | bytes accessed | tf_op | source)
XLA Modules:
  0.0 53.1 jit_solution(5292813560702455517)
XLA Ops:
  0.0 50.8 %shard_map.73 = bf16[128,4096]{1,0:T(8,128)(2,1)} custom-call(s32[8]{0:T(128)} %doc_ref.1, bf16[128,4096]{1,0:T(8,128)(2,1)} %hid.1, bf16[32,128,384]{2,1,0:T(8,128)(2,1)} %in_w.1, f32[3,12288]{1,0:T(4,128)} %feat_hbm.1, f32[7,4096]{1,0:T(8,128)} %inner_hbm.1, f32[1,4096]{1,0:T(1,128)} %bitcast.1, bf16[3,32,128,128]{3,2,1,0:T(8,128)(2,1)} %attn_w.1), custom_call_target="tpu_custom_call" | custom-call | flops 6000000000 | bytes 9000000 | tf_op jit(solution)/shard_map/pallas_call | solution.py:429
  50.8 2.3 %copy.9 = bf16[128,4096]{1,0:T(8,128)(2,1)} copy(bf16[128,4096]{1,0:T(8,128)(2,1)} %shard_map.73) | data formatting | bytes 2097152
